TPU v7x, 32 devices: a whole 2x2x4 slice. The times are simulated.
32 devices in a mesh: groups: 2 (over x), ep: 16 (over z, y, core).
Axes of the slice: x: 2, y: 2, z: 4, core: 2. Of those that a mesh axis runs over, the one named last changes fastest.
Arguments:
- query_proj: bfloat16 [8192, 4096], P(('groups', 'ep')), parts along dimension 0, may hold values from -8 to 8
- key_proj: bfloat16 [8192, 512], P(('groups', 'ep')), parts along dimension 0, may hold values from -8 to 8
- value_proj: bfloat16 [8192, 512], P(('groups', 'ep')), parts along dimension 0, may hold values from -6 to 6
- call_ids: int32 [8192], P(('groups', 'ep')), parts along dimension 0, may hold values from 0 to 15, never falling along the last dimension, each value on 1 to 1024 neighbouring positions
- sink_logits: float32 [64], replicated, may hold values from 2 to 6
- routed_stream: bfloat16 [512, 2880], P(('groups', 'ep')), parts along dimension 0, may hold values from -6 to 6
- expert_ids: int32 [512, 4], P(('groups', 'ep')), parts along dimension 0, may hold values from 0 to 7, as said below
- route_weights: float32 [512, 4], P(('groups', 'ep')), parts along dimension 0, may hold values from 0.1 to 1
- gate_up: bfloat16 [16, 2880, 2880], P('ep'), may hold values from -0.109375 to 0.109375
- down_proj: bfloat16 [16, 1440, 2880], P('ep'), may hold values from -0.109375 to 0.109375
Outputs:
- attended: bfloat16 [8192, 4096], P(('groups', 'ep')), parts along dimension 0
- expert_mix: bfloat16 [512, 2880], P(('groups', 'ep')), parts along dimension 0
There are 2 independent parts, one for each index of `groups`. A program takes and returns all parts, laid end to end along the dimension named above; an argument that names none is the same for every part. Nothing has to cross between parts.
Inputs may be any that keep to these rules, and one draw needn't show every extreme that they name: `expert_ids`: each row names 4 different experts. In each aligned block of 16 rows (the rows of one device) no expert is named by more than 12 rows, and some expert is named by exactly 12 rows in every block.
All inputs are finite; a program needn't handle non-finite values.
Results may differ from a plain program's by a relative error of at most 0.0058.
Values may be sent and summed in bfloat16 or wider, within the bound.
A program may use at most 128 MiB of HBM per device.

v0:
```python
import jax
import jax.numpy as jnp
from jax import lax
from jax.sharding import PartitionSpec as P

HD = 64
WINDOW = 128
EXPERTS = 8


def from_behind(value, axis, by):
    peers = lax.axis_size(axis)
    pairs = [(i, i + by) for i in range(peers) if 0 <= i + by < peers]
    return lax.ppermute(value, axis, pairs)


def window_attention(query_proj, key_value, query_calls, key_calls, sink_logits):
    length = query_proj.shape[0]
    extent = key_value.shape[0]
    feature_count = key_value.shape[1] // 2
    kv_heads = feature_count // HD
    group_size = sink_logits.shape[0] // kv_heads
    query_heads = query_proj.reshape(length, kv_heads, group_size, HD)
    key_heads = key_value[:, :feature_count].reshape(extent, kv_heads, HD)
    value_heads = key_value[:, feature_count:].reshape(extent, kv_heads, HD)
    scores = jnp.einsum(
        "tkgd,skd->kgts", query_heads, key_heads, preferred_element_type=jnp.float32
    ) * HD ** (-0.5)
    query_pos = jnp.arange(length, dtype=jnp.int32) + (extent - length)
    key_pos = jnp.arange(extent, dtype=jnp.int32)
    visible = (
        (key_pos[None, :] <= query_pos[:, None])
        & (query_pos[:, None] - key_pos[None, :] < WINDOW)
        & (key_calls[None, :] == query_calls[:, None])
    )
    scores = jnp.where(visible[None, None], scores, -1e30)
    sink_row = sink_logits.reshape(kv_heads, group_size)[:, :, None]
    largest = jnp.maximum(jnp.max(scores, axis=-1), sink_row)
    weights = jnp.where(visible[None, None], jnp.exp(scores - largest[..., None]), 0.0)
    denominator = jnp.sum(weights, axis=-1) + jnp.exp(sink_row - largest)
    rounded = weights.astype(jnp.bfloat16)
    blended = jnp.einsum("kgts,skd->tkgd", rounded, value_heads, preferred_element_type=jnp.float32)
    blended = blended / jnp.transpose(denominator, (2, 0, 1))[..., None]
    return blended.reshape(length, -1).astype(jnp.bfloat16)


def finish_expert(projected, weight_out):
    hidden_count = weight_out.shape[0]
    gate_part = projected[:, :hidden_count]
    up_part = projected[:, hidden_count:]
    activated = ((up_part + 1.0) * gate_part * jax.nn.sigmoid(1.702 * gate_part)).astype(
        jnp.bfloat16
    )
    return jnp.dot(activated, weight_out, preferred_element_type=jnp.float32).astype(jnp.bfloat16)


def on_device(
    query_proj,
    key_proj,
    value_proj,
    call_ids,
    sink_logits,
    routed_stream,
    expert_ids,
    route_weights,
    gate_up,
    down_proj,
):
    length = query_proj.shape[0]
    key_value = jnp.concatenate([key_proj, value_proj], axis=1)
    own_calls = call_ids + 1
    tail_kv, tail_calls = from_behind(
        (key_value[length - WINDOW :], own_calls[length - WINDOW :]), "ep", 1
    )
    window_kv = jnp.concatenate([tail_kv, key_value], axis=0)
    window_calls = jnp.concatenate([tail_calls, own_calls], axis=0)
    attended = window_attention(query_proj, window_kv, own_calls, window_calls, sink_logits)
    tokens = routed_stream.shape[0]
    feature_count = routed_stream.shape[1]
    topk_count = expert_ids.shape[1]
    holders = lax.axis_size("ep") // EXPERTS
    capacity = 3 * tokens * topk_count // (2 * EXPERTS)
    flat_ids = expert_ids.reshape(-1)
    owners = jnp.arange(EXPERTS, dtype=jnp.int32)
    onehot = (flat_ids[:, None] == owners[None, :]).astype(jnp.int32)
    pick_rank = jnp.sum((jnp.cumsum(onehot, axis=0) - onehot) * onehot, axis=1)
    slot_of = flat_ids * capacity + pick_rank
    token_of = jnp.arange(flat_ids.shape[0], dtype=jnp.int32) // topk_count
    sources = jnp.full((EXPERTS * capacity,), tokens, jnp.int32).at[slot_of].set(token_of)
    padded = jnp.concatenate(
        [routed_stream, jnp.zeros((1, feature_count), routed_stream.dtype)], axis=0
    )
    per_expert = padded[sources].reshape(EXPERTS, 1, capacity, feature_count)
    outgoing = jnp.broadcast_to(per_expert, (EXPERTS, holders, capacity, feature_count)).reshape(
        EXPERTS * holders, capacity, feature_count
    )
    weight_in = gate_up[0]
    weight_out = down_proj[0]
    received = lax.all_to_all(outgoing, "ep", split_axis=0, concat_axis=0, tiled=True)
    flat_rows = received.reshape(-1, feature_count)
    projected = jnp.dot(flat_rows, weight_in, preferred_element_type=jnp.float32)
    produced = finish_expert(projected, weight_out).reshape(received.shape)
    returned = lax.all_to_all(produced, "ep", split_axis=0, concat_axis=0, tiled=True)
    combined = jnp.sum(
        returned.reshape(EXPERTS, holders, capacity, feature_count).astype(jnp.float32), axis=1
    )
    picked = combined.reshape(-1, feature_count)[slot_of].reshape(tokens, topk_count, feature_count)
    expert_mix = jnp.sum(route_weights[..., None] * picked, axis=1).astype(jnp.bfloat16)
    return (attended, expert_mix)


def solution(mesh):
    in_specs = (
        P(("groups", "ep"), None),
        P(("groups", "ep"), None),
        P(("groups", "ep"), None),
        P(("groups", "ep")),
        P(),
        P(("groups", "ep"), None),
        P(("groups", "ep"), None),
        P(("groups", "ep"), None),
        P("ep", None, None),
        P("ep", None, None),
    )
    out_specs = (P(("groups", "ep"), None), P(("groups", "ep"), None))
    return jax.shard_map(
        on_device, mesh=mesh, in_specs=in_specs, out_specs=out_specs, check_vma=False
    )
```

profile of v0, /device:TPU:13, one launch (start us, length us, event | category | flops | bytes accessed | tf_op | source)
XLA Modules:
  0.0 115.0 jit_solution(2791871652514445790)
XLA Ops:
  0.6 1.0 constant_dynamic-update-slice_fusion.1
  1.6 1.0 constant_dynamic-update-slice_fusion
  2.6 0.7 slice.28
  3.3 3.7 %collective-permute-start = (bf16[128,1024]{1,0:T(8,128)(2,1)}, bf16[128,1024]{1,0:T(8,128)(2,1)}, u32[]{:S(2)}, u32[]{:S(2)}) collective-permute-start(bf16[128,1024]{1,0:T(8,128)(2,1)} %slice.28), channel_id=1, source_target_pairs={{0,1},{1,2},{2,3},{3,4},{4,5},{5,6},{6,7},{7,8},{8,9},{9,10},{10,1... | collective-permute-start | bytes 786440 | tf_op jit(solution)/shard_map/ppermute | solution.py:14
  7.0 0.7 broadcast_add_fusion
  7.7 1.9 %collective-permute-start.1 = (s32[128]{0:T(128)S(1)}, s32[128]{0:T(128)S(1)}, u32[]{:S(2)}, u32[]{:S(2)}) collective-permute-start(s32[128]{0:T(128)S(1)} %slice.20), channel_id=1, source_target_pairs={{0,1},{1,2},{2,3},{3,4},{4,5},{5,6},{6,7},{7,8},{8,9},{9,10},{10,1... | collective-permute-start | bytes 1544 | tf_op jit(solution)/shard_map/ppermute | solution.py:14
  9.6 0.7 broadcast_multiply_fusion
  10.3 0.8 copy.26
  11.1 0.1 copy.25
  11.2 0.1 mul.54
  11.2 0.1 eq.35
  11.3 0.1 fusion.25
  11.4 0.1 reduce_window_sum.11
  11.5 0.2 select_reduce_fusion
  11.7 0.8 scatter_custom_fusion
  12.5 0.9 concatenate.15
  13.4 0.9 gather_fusion
  14.3 0.1 broadcast_in_dim.51
  14.5 0.0 copy-start.1
  14.5 0.0 copy-start.4
  14.5 0.0 copy-start.3
  14.5 1.2 %broadcast_in_dim.52 = bf16[8,2,12,2880]{3,2,1,0:T(8,128)(2,1)} broadcast(bf16[8,12,2880]{2,1,0:T(8,128)(2,1)S(1)} %broadcast_in_dim.51), dimensions={0,2,3} | broadcast | bytes 1658880 | tf_op jit(solution)/shard_map/broadcast_in_dim | solution.py:94
  15.7 5.4 %all-to-all-start = ((bf16[16,12,2880]{2,1,0:T(8,128)(2,1)}), bf16[16,12,2880]{2,1,0:T(8,128)(2,1)}, u32[]{:S(2)}, u32[]{:S(2)}) async-start(bf16[16,12,2880]{2,1,0:T(8,128)(2,1)} %bitcast.13), calls=%async_computation | async-start | bytes 3014656 | tf_op jit(solution)/shard_map/all_to_all | solution.py:99
  21.2 0.0 copy-done.1
  21.2 2.5 %copy.22 = bf16[256,4096]{0,1:T(8,128)(2,1)} copy(bf16[256,4096]{1,0:T(8,128)(2,1)S(1)} %copy-done.1) | data formatting | bytes 4194304 | tf_op args[0]
  23.7 0.0 copy-done.4
  23.7 0.1 max.16
  23.7 0.0 copy-done.3
  23.7 0.1 copy.24
  23.8 0.0 collective-permute-done.1
  23.8 0.2 fusion.24
  24.0 0.0 collective-permute-done
  24.0 1.0 pad_maximum_fusion
  25.1 0.9 copy.20
  26.0 0.2 copy.21
  26.2 5.1 %fusion = (f32[8,8,256]{2,1,0:T(8,128)S(1)}, f32[8,384,256,8]{2,1,3,0:T(8,128)S(1)}) fusion(pred[256,384]{0,1:T(8,128)(4,1)S(1)} %fusion.24, bf16[384,8,64,1]{0,2,3,1:T(8,128)(2,1)S(1)} %bitcast.54, bf16[256,8,8,64]{0,3,2,1:T(8,128)(2,1)} %bitcast.53), kind=kOutput, calls=%fused_computation.5 | convolution fusion | flops 824164352 | bytes 27820032 | tf_op jit(solution)/shard_map/tkgd,skd->kgts/dot_general | solution.py:26
  31.3 0.0 copy-start
  31.3 0.1 broadcast_maximum_fusion
  31.4 7.3 %fusion.1 = f32[8,8,256]{2,1,0:T(8,128)S(1)} fusion(f32[8,384,256,8]{2,1,3,0:T(8,128)S(1)} %get-tuple-element.9, f32[8,8,256]{2,1,0:T(8,128)S(1)} %broadcast_maximum_fusion, pred[256,384]{0,1:T(8,128)(4,1)S(1)} %fusion.24), kind=kLoop, calls=%fused_computation.6 | loop fusion | flops 31440896 | bytes 25395200 | tf_op jit(solution)/shard_map/reduce_sum | solution.py:40
  38.7 0.9 copy-done
  39.6 0.1 add_bitcast_fusion
  39.7 16.4 %all-to-all-done = bf16[16,12,2880]{2,1,0:T(8,128)(2,1)} async-done(((bf16[16,12,2880]{2,1,0:T(8,128)(2,1)}), bf16[16,12,2880]{2,1,0:T(8,128)(2,1)}, u32[]{:S(2)}, u32[]{:S(2)}) %all-to-all-start) | async-done | bytes 1105952 | tf_op jit(solution)/shard_map/all_to_all | solution.py:99
  56.1 1.7 %reshape.147 = bf16[192,2880]{1,0:T(8,128)(2,1)S(1)} reshape(bf16[16,12,2880]{2,1,0:T(8,128)(2,1)} %all-to-all-done) | data formatting | bytes 2211840 | tf_op jit(solution)/shard_map/reshape | solution.py:100
  57.7 7.9 %fusion.3 = f32[192,2880]{1,0:T(8,128)S(1)} fusion(bf16[192,2880]{1,0:T(8,128)(2,1)S(1)} %reshape.147, bf16[1,2880,2880]{2,1,0:T(8,128)(2,1)} %param.18), kind=kOutput, calls=%fused_computation.8 | convolution fusion | flops 3185049600 | bytes 19906560 | tf_op jit(solution)/shard_map/dot_general | solution.py:101
  65.6 5.6 %fusion.11 = bf16[192,2880]{1,0:T(8,128)(2,1)S(1)} fusion(bf16[1,1440,2880]{2,1,0:T(8,128)(2,1)} %param.19, f32[192,2880]{1,0:T(8,128)S(1)} %fusion.3), kind=kOutput, calls=%fused_computation.16 | convolution fusion | flops 1595289600 | bytes 11759616 | tf_op jit(solution)/shard_map/dot_general | solution.py:54
  71.2 0.0 copy-start.2
  71.2 1.4 %reshape.148 = bf16[16,12,2880]{2,1,0:T(8,128)(2,1)} reshape(bf16[192,2880]{1,0:T(8,128)(2,1)S(1)} %fusion.11) | data formatting | bytes 2211840 | tf_op jit(solution)/shard_map/reshape | solution.py:102
  72.6 4.9 %all-to-all-start.1 = ((bf16[16,12,2880]{2,1,0:T(8,128)(2,1)}), bf16[16,12,2880]{2,1,0:T(8,128)(2,1)S(1)}, u32[]{:S(2)}, u32[]{:S(2)}) async-start(bf16[16,12,2880]{2,1,0:T(8,128)(2,1)} %reshape.148), calls=%async_computation.1 | async-start | bytes 3014656 | tf_op jit(solution)/shard_map/all_to_all | solution.py:103
  77.5 0.0 copy-done.2
  77.5 12.3 %fusion.10 = bf16[256,8,8,64]{0,3,2,1:T(8,128)(2,1)} fusion(bf16[384,8,64,1]{0,2,3,1:T(8,128)(2,1)S(1)} %bitcast.56, f32[8,384,256,8]{2,1,3,0:T(8,128)} %copy-done, f32[8,8,256]{2,1,0:T(8,128)S(1)} %broadcast_maximum_fusion, pred[256,384]{0,1:T(8,128)(4,1)S(1)} %fusion.24, f32[256,8,8]{0,2,1:T(8,128)S(1)} %add_bitcast_fusion), kind=kOutput, calls=%fused_computation.15 | convolution fusion | flops 838860800 | bytes 27885568 | tf_op jit(solution)/shard_map/kgts,skd->tkgd/dot_general | solution.py:42
  89.8 4.1 %copy.27 = bf16[256,4096]{1,0:T(8,128)(2,1)} copy(bf16[256,4096]{0,1:T(8,128)(2,1)} %bitcast.55) | data formatting | bytes 4194304
  93.9 18.5 %all-to-all-done.1 = bf16[16,12,2880]{2,1,0:T(8,128)(2,1)S(1)} async-done(((bf16[16,12,2880]{2,1,0:T(8,128)(2,1)}), bf16[16,12,2880]{2,1,0:T(8,128)(2,1)S(1)}, u32[]{:S(2)}, u32[]{:S(2)}) %all-to-all-start.1) | async-done | bytes 1105952 | tf_op jit(solution)/shard_map/all_to_all | solution.py:103
  112.3 0.3 convert_reduce_fusion
  112.6 0.1 reshape.149
  112.7 0.8 gather_fusion.1
  113.6 0.2 reshape.150
  113.8 1.2 %multiply_reduce_fusion = bf16[16,2880]{1,0:T(8,128)(2,1)} fusion(f32[16,4,2880]{2,1,0:T(4,128)S(1)} %reshape.150, f32[16,4]{1,0:T(8,128)S(1)} %copy.24), kind=kLoop, calls=%fused_computation.24 | loop fusion | flops 322560 | bytes 829696 | tf_op jit(solution)/shard_map/reduce_sum | solution.py:108
  (8 shorter events, 0.0 us)
Async XLA Ops:
  3.3 20.7 %collective-permute-start = (bf16[128,1024]{1,0:T(8,128)(2,1)}, bf16[128,1024]{1,0:T(8,128)(2,1)}, u32[]{:S(2)}, u32[]{:S(2)}) collective-permute-start(bf16[128,1024]{1,0:T(8,128)(2,1)} %slice.28), channel_id=1, source_target_pairs={{0,1},{1,2},{2,3},{3,4},{4,5},{5,6},{6,7},{7,8},{8,9},{9,10},{10,1... | collective-permute-start | bytes 786440 | tf_op jit(solution)/shard_map/ppermute | solution.py:14
  7.7 16.1 %collective-permute-start.1 = (s32[128]{0:T(128)S(1)}, s32[128]{0:T(128)S(1)}, u32[]{:S(2)}, u32[]{:S(2)}) collective-permute-start(s32[128]{0:T(128)S(1)} %slice.20), channel_id=1, source_target_pairs={{0,1},{1,2},{2,3},{3,4},{4,5},{5,6},{6,7},{7,8},{8,9},{9,10},{10,1... | collective-permute-start | bytes 1544 | tf_op jit(solution)/shard_map/ppermute | solution.py:14
  14.5 6.7 %copy-start.1 = (bf16[256,4096]{1,0:T(8,128)(2,1)S(1)}, bf16[256,4096]{1,0:T(8,128)(2,1)}, u32[]{:S(2)}) copy-start(bf16[256,4096]{1,0:T(8,128)(2,1)} %param.10) | copy-start | bytes 6291460
  14.5 9.2 %copy-start.4 = (f32[64]{0:T(128)S(1)}, f32[64]{0:T(128)}, u32[]{:S(2)}) copy-start(f32[64]{0:T(128)} %param.14) | copy-start | bytes 772
  14.5 9.2 %copy-start.3 = (f32[16,4]{0,1:T(4,128)S(1)}, f32[16,4]{0,1:T(4,128)}, u32[]{:S(2)}) copy-start(f32[16,4]{0,1:T(4,128)} %param.17) | copy-start | bytes 772
  15.7 40.3 %all-to-all-start = ((bf16[16,12,2880]{2,1,0:T(8,128)(2,1)}), bf16[16,12,2880]{2,1,0:T(8,128)(2,1)}, u32[]{:S(2)}, u32[]{:S(2)}) async-start(bf16[16,12,2880]{2,1,0:T(8,128)(2,1)} %bitcast.13), calls=%async_computation | async-start | bytes 3014656 | tf_op jit(solution)/shard_map/all_to_all | solution.py:99
  31.3 8.3 %copy-start = (f32[8,384,256,8]{2,1,3,0:T(8,128)}, f32[8,384,256,8]{2,1,3,0:T(8,128)S(1)}, u32[]{:S(2)}) copy-start(f32[8,384,256,8]{2,1,3,0:T(8,128)S(1)} %get-tuple-element.9) | copy-start | bytes 75497472
  71.2 6.3 %copy-start.2 = (bf16[384,512]{0,1:T(8,128)(2,1)S(1)}, bf16[384,512]{0,1:T(8,128)(2,1)}, u32[]{:S(2)}) copy-start(bf16[384,512]{0,1:T(8,128)(2,1)} %copy.20) | copy-start | bytes 1179652
  72.6 39.7 %all-to-all-start.1 = ((bf16[16,12,2880]{2,1,0:T(8,128)(2,1)}), bf16[16,12,2880]{2,1,0:T(8,128)(2,1)S(1)}, u32[]{:S(2)}, u32[]{:S(2)}) async-start(bf16[16,12,2880]{2,1,0:T(8,128)(2,1)} %reshape.148), calls=%async_computation.1 | async-start | bytes 3014656 | tf_op jit(solution)/shard_map/all_to_all | solution.py:103
where the time goes:
time: 116 us; the launch traced here: 115 us
  waiting for transfers between devices  34.8 us (30%)
  matrix products  30.8 us (27%)
  local copies, waits for them, and re-layouts  20.7 us (18%)
  starting transfers between devices  15.9 us (14%)
  other arithmetic  11.9 us (10%)
    all_to_all x1, waiting for transfers between devices, on_device(): lax.all_to_all(produced, 'ep', split_axis=0, concat_axis=0, tiled=True)  18.5 us
    all_to_all x1, waiting for transfers between devices, on_device(): lax.all_to_all(outgoing, 'ep', split_axis=0, concat_axis=0, tiled=True)  16.4 us
    dot_general x1, matrix products, window_attention(): jnp.einsum('kgts,skd->tkgd', rounded, value_heads, preferred_element_type...  12.3 us
    unnamed x15, local copies, waits for them, and re-layouts  9.27 us
    dot_general x1, matrix products, on_device(): jnp.dot(flat_rows, weight_in, preferred_element_type=jnp.float32)  7.87 us
    reduce_sum x1, other arithmetic, window_attention(): denominator = jnp.sum(weights, axis=-1) + jnp.exp(sink_row - largest)  7.3 us
    ppermute x2, starting transfers between devices, from_behind(): return lax.ppermute(value, axis, pairs)  5.61 us
    dot_general x1, matrix products, finish_expert(): jnp.dot(activated, weight_out, preferred_element_type=jnp.float32)  5.58 us
  transfers between devices with their start and end apart: 4, of which 2 were waited for; matrix products, arithmetic and copies ran while one was open for 35% of the time, Pallas kernels for 0%

commit v1 on v0

v1 whole, which is shorter than its diff:
```python
import functools

import jax
import jax.numpy as jnp
from jax import lax
from jax.experimental import pallas as pl
from jax.experimental.pallas import tpu as pltpu
from jax.sharding import PartitionSpec as P

HD = 64
WINDOW = 128
EXPERTS = 8
LANES = 128
TILE = 256
F32 = jnp.float32
BF16 = jnp.bfloat16


def up_to(value, unit):
    return -(-value // unit) * unit


def cuts(total, width):
    return [(at, min(width, total - at)) for at in range(0, total, width)]


def row_parts(rows, parts):
    step = up_to(-(-rows // parts), 16)
    return cuts(rows, step)


def kernel(
    n,
    q_hbm,
    k_hbm,
    v_hbm,
    calls_ref,
    sink_ref,
    routed_ref,
    ids_ref,
    route_ref,
    gate_hbm,
    down_hbm,
    att_hbm,
    mix_ref,
    q_buf,
    o_buf,
    k_cat,
    v_cat,
    calls_in,
    calls_out,
    bias,
    tokens,
    w_in,
    w_out,
    hidden,
    act,
    mine,
    s1,
    r1,
    acc2,
    s2,
    r2,
    acc3,
    s3,
    r3,
    load_sem,
    gate_sem,
    down_sem,
    halo_send,
    halo_recv,
    z_send,
    y_send,
    c_send,
    slot_recv,
    s1_send,
    s1_recv,
    s2_send,
    s2_recv,
    s3_send,
    s3_recv,
    out_sem,
):
    zs = n // 4
    me = lax.axis_index("ep")
    core, row, z = me % 2, (me // 2) % 2, me // 4
    sibling = me + 1 - 2 * core
    across = me + 2 - 4 * row
    ahead, behind = (me + 1) % n, (me + n - 1) % n

    def along(by):
        return ((z + by) % zs) * 4 + row * 2 + core

    length = q_hbm.shape[0]
    block = length // 2
    count, d = routed_ref.shape
    dp = tokens.shape[1]
    fe = down_hbm.shape[0]
    half = zs * 2 * count
    quarter = zs * count

    barrier = pltpu.get_barrier_semaphore()
    for peer in [sibling, across, ahead, behind] + [along(k) for k in range(1, zs)]:
        pl.semaphore_signal(
            barrier, inc=1, device_id={"ep": peer}, device_id_type=pl.DeviceIdType.MESH
        )

    def remote(src, dst, send, recv, peer):
        return pltpu.make_async_remote_copy(
            src_ref=src,
            dst_ref=dst,
            send_sem=send,
            recv_sem=recv,
            device_id={"ep": peer},
            device_id_type=pl.DeviceIdType.MESH,
        )

    loads = [
        pltpu.make_async_copy(k_hbm, k_cat.at[pl.ds(WINDOW, length)], load_sem.at[0]),
        pltpu.make_async_copy(v_hbm, v_cat.at[pl.ds(WINDOW, length)], load_sem.at[1]),
        pltpu.make_async_copy(
            q_hbm.at[pl.ds(block, block)], q_buf.at[pl.ds(block, block)], load_sem.at[2]
        ),
        pltpu.make_async_copy(
            q_hbm.at[pl.ds(0, block)], q_buf.at[pl.ds(0, block)], load_sem.at[3]
        ),
    ]
    for copy in loads:
        copy.start()
    gate_loads = [
        pltpu.make_async_copy(
            gate_hbm.at[pl.ds(at, size)], w_in.at[pl.ds(at, size)], gate_sem.at[i]
        )
        for i, (at, size) in enumerate(row_parts(d, 4))
    ]
    down_loads = [
        pltpu.make_async_copy(
            down_hbm.at[pl.ds(at, size)], w_out.at[pl.ds(at, size)], down_sem.at[i]
        )
        for i, (at, size) in enumerate(row_parts(fe, 2))
    ]
    for copy in gate_loads + down_loads:
        copy.start()

    ids = ids_ref[...]
    route = route_ref[...]
    lane = lax.broadcasted_iota(jnp.int32, (count, LANES), 1)
    last = dp - LANES
    free = d - last
    extra = jnp.zeros((count, LANES), F32)
    for e in range(EXPERTS):
        weight = jnp.sum(jnp.where(ids == e, route, 0.0), axis=1, keepdims=True)
        high = weight.astype(BF16).astype(F32)
        extra = jnp.where(lane == free + e, high, extra)
        extra = jnp.where(lane == free + EXPERTS + e, weight - high, extra)
    tokens[0:count, 0:d] = routed_ref[...]
    tail = tokens[0:count, last:dp].astype(F32)
    tokens[0:count, last:dp] = jnp.where(lane < free, tail, extra).astype(BF16)
    own_calls = calls_ref[...]
    calls_out[...] = jnp.broadcast_to(own_calls[:, length - WINDOW :], calls_out.shape)

    pl.semaphore_wait(barrier, zs + 3)

    def slot(cr, yr, zr):
        return tokens.at[pl.ds(((cr * 2 + yr) * zs + zr) * count, count)]

    def arrival(cr, yr, zr):
        return slot_recv.at[(cr * 2 + yr) * zs + zr]

    sent = []

    def send(*args):
        copy = remote(*args)
        copy.start()
        sent.append(copy)

    def arrived(ref, sem):
        pltpu.make_async_copy(ref, ref, sem).wait()

    for k in range(1, zs):
        send(slot(0, 0, 0), slot(0, 0, zs - k), z_send.at[k - 1], arrival(0, 0, zs - k), along(k))
    send(slot(0, 0, 0), slot(0, 1, 0), y_send.at[0], arrival(0, 1, 0), across)
    send(slot(0, 0, 0), slot(1, 0, 0), c_send.at[0], arrival(1, 0, 0), sibling)
    edge = pl.ds(length - WINDOW, WINDOW)
    head = pl.ds(0, WINDOW)
    send(k_hbm.at[edge], k_cat.at[head], halo_send.at[0], halo_recv.at[0], ahead)
    send(v_hbm.at[edge], v_cat.at[head], halo_send.at[1], halo_recv.at[1], ahead)
    send(calls_out, calls_in, halo_send.at[2], halo_recv.at[2], ahead)

    def make_bias(index, key_calls, query_calls, behind_ok):
        query = lax.broadcasted_iota(jnp.int32, (block, WINDOW + block), 0)
        key = lax.broadcasted_iota(jnp.int32, (block, WINDOW + block), 1)
        spread = jnp.broadcast_to(query_calls, (block, block))
        diag = lax.broadcasted_iota(jnp.int32, (block, block), 0) == lax.broadcasted_iota(
            jnp.int32, (block, block), 1
        )
        column = jnp.sum(
            jnp.where(diag, spread.astype(F32), 0.0), axis=1, keepdims=True
        ).astype(jnp.int32)
        seen = (key <= query + WINDOW) & (key > query) & (key_calls == column)
        if behind_ok is not None:
            seen = seen & ((key >= WINDOW) | behind_ok)
        bias[index] = jnp.where(seen, 0.0, -1e30)

    def attend(index, first, stop):
        base = index * block
        span = WINDOW + block

        def body(gp, carry):
            columns = pl.ds(pl.multiple_of(gp * LANES, LANES), LANES)
            k2 = k_cat[base : base + span, columns].astype(F32) * HD ** (-0.5)
            v2 = v_cat[base : base + span, columns].astype(F32)
            low = lax.broadcasted_iota(jnp.int32, (span, LANES), 1) < HD
            low_out = lax.broadcasted_iota(jnp.int32, (block, LANES), 1) < HD
            ones_low = jnp.where(low, 1.0, 0.0)
            ones_high = 1.0 - ones_low
            for side in range(2):
                keep = low if side == 0 else jnp.logical_not(low)
                ka = jnp.where(keep, k2, 0.0)
                kb = pltpu.roll(ka, HD, 1)
                va = jnp.where(keep, v2, 0.0)
                vb = pltpu.roll(va, HD, 1)
                if side:
                    ka, kb, va, vb = kb, ka, vb, va
                keys = jnp.concatenate([ka, kb], axis=0).astype(BF16)
                values = jnp.concatenate(
                    [
                        jnp.concatenate([va, ones_low], axis=1),
                        jnp.concatenate([vb, ones_high], axis=1),
                    ],
                    axis=0,
                ).astype(BF16)
                for pair in range(4):
                    at = pl.multiple_of(gp * (16 * HD) + (side * 8 + pair * 2) * HD, LANES)
                    q2 = q_buf[base : base + block, pl.ds(at, LANES)]
                    scores = lax.dot_general(
                        q2, keys, (((1,), (1,)), ((), ())), preferred_element_type=F32
                    )
                    seen = bias[index]
                    weights, sinks = [], []
                    for one in range(2):
                        sink = sink_ref[gp * 16 + side * 8 + pair * 2 + one]
                        part = scores[:, one * span : (one + 1) * span] + seen
                        largest = jnp.maximum(jnp.max(part, axis=1, keepdims=True), sink)
                        weights.append(jnp.exp(part - largest))
                        sinks.append(jnp.exp(sink - largest))
                    both = jnp.concatenate(weights, axis=1).astype(BF16)
                    mixed = jnp.dot(both, values, preferred_element_type=F32)
                    bottom = mixed[:, LANES:] + jnp.where(low_out, sinks[0], sinks[1])
                    o_buf[base : base + block, pl.ds(at, LANES)] = (
                        mixed[:, :LANES] / bottom
                    ).astype(BF16)
            return carry

        lax.fori_loop(first, stop, body, 0)

    groups = k_hbm.shape[1] // LANES
    make_bias(1, own_calls, own_calls[:, block:], None)
    for copy in loads[:3]:
        copy.wait()
    attend(1, 0, groups // 2)
    for k in range(1, zs):
        arrived(slot(0, 0, zs - k), arrival(0, 0, zs - k))
        send(slot(0, 0, zs - k), slot(0, 1, zs - k), y_send.at[k], arrival(0, 1, zs - k), across)
        send(slot(0, 0, zs - k), slot(1, 0, zs - k), c_send.at[k], arrival(1, 0, zs - k), sibling)
    attend(1, groups // 2, groups)
    store_late = pltpu.make_async_copy(
        o_buf.at[pl.ds(block, block)], att_hbm.at[pl.ds(block, block)], out_sem.at[0]
    )
    store_late.start()
    for k in range(zs):
        zr = (zs - k) % zs
        arrived(slot(0, 1, zr), arrival(0, 1, zr))
        send(slot(0, 1, zr), slot(1, 1, zr), c_send.at[zs + k], arrival(1, 1, zr), sibling)
    for copy in gate_loads + down_loads:
        copy.wait()
    loads[3].wait()
    arrived(k_cat.at[head], halo_recv.at[0])
    arrived(v_cat.at[head], halo_recv.at[1])
    arrived(calls_in, halo_recv.at[2])
    make_bias(
        0,
        jnp.concatenate([calls_in[0:1, :], own_calls[:, :block]], axis=1),
        own_calls[:, :block],
        me > 0,
    )
    for yr in range(2):
        for zr in range(zs):
            arrived(slot(1, yr, zr), arrival(1, yr, zr))

    rows = n * count

    def project(at, size):
        hidden[:, pl.ds(at, size)] = jnp.dot(
            tokens[:, 0:d], w_in[:, pl.ds(at, size)], preferred_element_type=F32
        )

    whole = (2 * fe) // TILE
    lax.fori_loop(
        0, whole, lambda i, c: (project(pl.multiple_of(i * TILE, TILE), TILE), c)[1], 0
    )
    if 2 * fe > whole * TILE:
        project(whole * TILE, 2 * fe - whole * TILE)
    off = fe % LANES
    for at, size in cuts(up_to(fe, LANES), TILE):
        gate = hidden[:, at : at + size]
        up = hidden[:, fe - off + at : fe - off + at + size + LANES]
        if off:
            up = pltpu.roll(up, size + LANES - off, 1)
        up = up[:, :size]
        act[:, at : at + size] = ((up + 1.0) * gate * jax.nn.sigmoid(1.702 * gate)).astype(BF16)
    lane = lax.broadcasted_iota(jnp.int32, (rows, LANES), 1)
    expert = me // (n // EXPERTS)
    picked = (lane == free + expert) | (lane == free + EXPERTS + expert)
    share = jnp.sum(
        jnp.where(picked, tokens[:, last:dp].astype(F32), 0.0), axis=1, keepdims=True
    )

    pieces = cuts(d, 6 * LANES)

    def stage1(j):
        at, size = pieces[j]
        cols = pl.ds(at, size)
        result = (
            jnp.dot(act[:, 0:fe], w_out[:, cols], preferred_element_type=F32) * share
        )
        mine[:, cols] = result[:half]
        s1[:, cols] = result[half:].astype(BF16)
        span = pl.ds(at, up_to(size, LANES))
        send(s1.at[:, span], r1.at[:, span], s1_send.at[j], s1_recv.at[j], sibling)

    def stage2(j):
        at, size = pieces[j]
        cols = pl.ds(at, size)
        span = pl.ds(at, up_to(size, LANES))
        arrived(r1.at[:, span], s1_recv.at[j])
        total = mine[:, cols] + r1[:, cols].astype(F32)
        acc2[:, cols] = total[:quarter]
        s2[:, cols] = total[quarter:].astype(BF16)
        send(s2.at[:, span], r2.at[:, span], s2_send.at[j], s2_recv.at[j], across)

    def stage3(j):
        at, size = pieces[j]
        cols = pl.ds(at, size)
        span = pl.ds(at, up_to(size, LANES))
        arrived(r2.at[:, span], s2_recv.at[j])
        total = acc2[:, cols] + r2[:, cols].astype(F32)
        acc3[:, cols] = total[:count]
        s3[:, cols] = total.astype(BF16)
        for k in range(1, zs):
            there = pl.ds(k * count, count)
            index = j * (zs - 1) + k - 1
            send(
                s3.at[there, span], r3.at[there, span], s3_send.at[index], s3_recv.at[index], along(k)
            )

    def stage4(j):
        at, size = pieces[j]
        cols = pl.ds(at, size)
        span = pl.ds(at, up_to(size, LANES))
        total = acc3[:, cols]
        for k in range(1, zs):
            there = pl.ds(k * count, count)
            arrived(r3.at[there, span], s3_recv.at[j * (zs - 1) + k - 1])
            total = total + r3[there, cols].astype(F32)
        mix_ref[:, cols] = total.astype(BF16)

    for j in range(len(pieces)):
        stage1(j)
        if j:
            stage2(j - 1)
    stage2(len(pieces) - 1)
    steps = len(pieces)
    done = 0
    for g in range(groups // 2):
        attend(0, 2 * g, 2 * g + 2)
        upto = steps * (g + 1) // (groups // 2)
        for j in range(done, upto):
            stage3(j)
        done = upto
    store_early = pltpu.make_async_copy(
        o_buf.at[pl.ds(0, block)], att_hbm.at[pl.ds(0, block)], out_sem.at[1]
    )
    store_early.start()
    for j in range(steps):
        stage4(j)
    for copy in sent:
        copy.wait_send()
    store_late.wait()
    store_early.wait()


def on_device(
    n,
    query_proj,
    key_proj,
    value_proj,
    call_ids,
    sink_logits,
    routed_stream,
    expert_ids,
    route_weights,
    gate_up,
    down_proj,
):
    length = query_proj.shape[0]
    block = length // 2
    kv = key_proj.shape[1]
    count, d = routed_stream.shape
    dp = up_to(d + 2 * EXPERTS, LANES)
    fe = down_proj.shape[1]
    rows = n * count
    zs = n // 4
    wide = (fe // LANES) * LANES + up_to(fe, TILE) + LANES
    pieces = len(cuts(d, 6 * LANES))
    vmem = pl.BlockSpec(memory_space=pltpu.VMEM)
    smem = pl.BlockSpec(memory_space=pltpu.SMEM)
    hbm = pl.BlockSpec(memory_space=pl.ANY)
    dma = pltpu.SemaphoreType.DMA
    return pl.pallas_call(
        functools.partial(kernel, n),
        out_shape=(
            jax.ShapeDtypeStruct(query_proj.shape, BF16),
            jax.ShapeDtypeStruct(routed_stream.shape, BF16),
        ),
        in_specs=[hbm, hbm, hbm, vmem, smem, vmem, vmem, vmem, hbm, hbm],
        out_specs=(hbm, vmem),
        scratch_shapes=[
            pltpu.VMEM(query_proj.shape, BF16),
            pltpu.VMEM(query_proj.shape, BF16),
            pltpu.VMEM((WINDOW + length, kv), BF16),
            pltpu.VMEM((WINDOW + length, kv), BF16),
            pltpu.VMEM((8, WINDOW), jnp.int32),
            pltpu.VMEM((8, WINDOW), jnp.int32),
            pltpu.VMEM((2, block, WINDOW + block), F32),
            pltpu.VMEM((rows, dp), BF16),
            pltpu.VMEM(gate_up.shape[1:], BF16),
            pltpu.VMEM(down_proj.shape[1:], BF16),
            pltpu.VMEM((rows, wide), F32),
            pltpu.VMEM((rows, up_to(fe, TILE)), BF16),
            pltpu.VMEM((rows // 2, dp), F32),
            pltpu.VMEM((rows // 2, dp), BF16),
            pltpu.VMEM((rows // 2, dp), BF16),
            pltpu.VMEM((rows // 4, dp), F32),
            pltpu.VMEM((rows // 4, dp), BF16),
            pltpu.VMEM((rows // 4, dp), BF16),
            pltpu.VMEM((count, dp), F32),
            pltpu.VMEM((rows // 4, dp), BF16),
            pltpu.VMEM((rows // 4, dp), BF16),
            dma((4,)),
            dma((4,)),
            dma((2,)),
            dma((3,)),
            dma((3,)),
            dma((zs - 1,)),
            dma((zs,)),
            dma((2 * zs,)),
            dma((4 * zs,)),
            dma((pieces,)),
            dma((pieces,)),
            dma((pieces,)),
            dma((pieces,)),
            dma((pieces * (zs - 1),)),
            dma((pieces * (zs - 1),)),
            dma((2,)),
        ],
        compiler_params=pltpu.CompilerParams(
            collective_id=0, has_side_effects=True, vmem_limit_bytes=58 * 2**20
        ),
    )(
        query_proj,
        key_proj,
        value_proj,
        call_ids.reshape(1, length),
        sink_logits,
        routed_stream,
        expert_ids,
        route_weights,
        gate_up[0],
        down_proj[0],
    )


def solution(mesh):
    in_specs = (
        P(("groups", "ep"), None),
        P(("groups", "ep"), None),
        P(("groups", "ep"), None),
        P(("groups", "ep")),
        P(),
        P(("groups", "ep"), None),
        P(("groups", "ep"), None),
        P(("groups", "ep"), None),
        P("ep", None, None),
        P("ep", None, None),
    )
    out_specs = (P(("groups", "ep"), None), P(("groups", "ep"), None))
    return jax.shard_map(
        functools.partial(on_device, mesh.shape["ep"]),
        mesh=mesh,
        in_specs=in_specs,
        out_specs=out_specs,
        check_vma=False,
    )
```

time: 116 us -> 57 us (0.49)
  the two profiles are of different devices: /device:TPU:13 before, /device:TPU:0 now
where the time goes in v1:
time: 57 us; the launch traced here: 56.7 us
  Pallas kernels  49.6 us (87%)
  local copies, waits for them, and re-layouts  6.52 us (11%)
  between operations  0.65 us (1%)
    pallas_call x1, Pallas kernels, on_device(): pl.pallas_call(functools.partial(kernel, n), out_shape=(jax.ShapeDtypeStr...  49.6 us
    unnamed x6, local copies, waits for them, and re-layouts  6.52 us

profile of v1, /device:TPU:0, one launch (start us, length us, event | category | flops | bytes accessed | tf_op | source)
XLA Modules:
  0.0 56.7 jit_solution(16234132058414651021)
XLA Ops:
  0.6 1.4 %copy.12.ids_ref = s32[16,4]{1,0:T(8,128)} copy(s32[16,4]{0,1:T(4,128)} %param.16) | data formatting | bytes 512 | tf_op args[6]
  2.0 1.4 %copy.13.route_ref = f32[16,4]{1,0:T(8,128)} copy(f32[16,4]{0,1:T(4,128)} %param.17) | data formatting | bytes 512 | tf_op args[7]
  3.3 49.6 %shard_map.113 = (bf16[256,4096]{1,0:T(8,128)(2,1)}, bf16[16,2880]{1,0:T(8,128)(2,1)}) custom-call(bf16[256,4096]{1,0:T(8,128)(2,1)} %q_hbm.1, bf16[256,512]{1,0:T(8,128)(2,1)} %k_hbm.1, bf16[256,512]{1,0:T(8,128)(2,1)} %v_hbm.1, s32[1,256]{1,0:T(1,128)} %bitcast.5, f32[64]{0:T(128)} %sink_ref.1, bf16[16,2880]{1,0:T(8,128)(2,1)} %routed_ref.1, ...), custom_call_target="tpu_custom_call" | custom-call | tf_op jit(solution)/shard_map/pallas_call | solution.py:420
  52.9 0.0 copy-start
  52.9 3.2 %copy.16 = bf16[256,4096]{1,0:T(8,128)(2,1)} copy(bf16[256,4096]{1,0:T(8,128)(2,1)} %get-tuple-element.4) | data formatting | bytes 4194304
  56.1 0.0 copy-done
  56.1 0.6 %copy.17 = bf16[16,2880]{1,0:T(8,128)(2,1)} copy(bf16[16,2880]{1,0:T(8,128)(2,1)S(1)} %copy-done) | data formatting | bytes 184320
Async XLA Ops:
  52.9 3.2 %copy-start = (bf16[16,2880]{1,0:T(8,128)(2,1)S(1)}, bf16[16,2880]{1,0:T(8,128)(2,1)}, u32[]{:S(2)}) copy-start(bf16[16,2880]{1,0:T(8,128)(2,1)} %get-tuple-element.5) | copy-start | bytes 276484

commit v2 on v1

--- a/solution.py
+++ b/solution.py
@@ -41,10 +41,9 @@
     route_ref,
     gate_hbm,
     down_hbm,
-    att_hbm,
+    o_buf,
     mix_ref,
     q_buf,
-    o_buf,
     k_cat,
     v_cat,
     calls_in,
@@ -79,7 +78,6 @@
     s2_recv,
     s3_send,
     s3_recv,
-    out_sem,
 ):
     zs = n // 4
     me = lax.axis_index("ep")
@@ -139,17 +137,25 @@
         )
         for i, (at, size) in enumerate(row_parts(fe, 2))
     ]
-    for copy in gate_loads + down_loads:
-        copy.start()
-
-    ids = ids_ref[...]
+
+    topk = ids_ref.shape[0]
+    square = lax.broadcasted_iota(jnp.int32, (count, count), 0) == lax.broadcasted_iota(
+        jnp.int32, (count, count), 1
+    )
+    ids = ids_ref[...].astype(F32)
     route = route_ref[...]
+
+    def column(values, k):
+        spread = jnp.broadcast_to(values[k : k + 1, :], (count, count))
+        return jnp.sum(jnp.where(square, spread, 0.0), axis=1, keepdims=True)
+
+    chosen = [(column(ids, k), column(route, k)) for k in range(topk)]
     lane = lax.broadcasted_iota(jnp.int32, (count, LANES), 1)
     last = dp - LANES
     free = d - last
     extra = jnp.zeros((count, LANES), F32)
     for e in range(EXPERTS):
-        weight = jnp.sum(jnp.where(ids == e, route, 0.0), axis=1, keepdims=True)
+        weight = sum(jnp.where(i == float(e), w, 0.0) for i, w in chosen)
         high = weight.astype(BF16).astype(F32)
         extra = jnp.where(lane == free + e, high, extra)
         extra = jnp.where(lane == free + EXPERTS + e, weight - high, extra)
@@ -186,6 +192,9 @@
     send(k_hbm.at[edge], k_cat.at[head], halo_send.at[0], halo_recv.at[0], ahead)
     send(v_hbm.at[edge], v_cat.at[head], halo_send.at[1], halo_recv.at[1], ahead)
     send(calls_out, calls_in, halo_send.at[2], halo_recv.at[2], ahead)
+
+    for copy in gate_loads + down_loads:
+        copy.start()
 
     def make_bias(index, key_calls, query_calls, behind_ok):
         query = lax.broadcasted_iota(jnp.int32, (block, WINDOW + block), 0)
@@ -264,10 +273,6 @@
         send(slot(0, 0, zs - k), slot(0, 1, zs - k), y_send.at[k], arrival(0, 1, zs - k), across)
         send(slot(0, 0, zs - k), slot(1, 0, zs - k), c_send.at[k], arrival(1, 0, zs - k), sibling)
     attend(1, groups // 2, groups)
-    store_late = pltpu.make_async_copy(
-        o_buf.at[pl.ds(block, block)], att_hbm.at[pl.ds(block, block)], out_sem.at[0]
-    )
-    store_late.start()
     for k in range(zs):
         zr = (zs - k) % zs
         arrived(slot(0, 1, zr), arrival(0, 1, zr))
@@ -316,7 +321,7 @@
         jnp.where(picked, tokens[:, last:dp].astype(F32), 0.0), axis=1, keepdims=True
     )
 
-    pieces = cuts(d, 6 * LANES)
+    pieces = cuts(d, 12 * LANES)
 
     def stage1(j):
         at, size = pieces[j]
@@ -378,16 +383,10 @@
         for j in range(done, upto):
             stage3(j)
         done = upto
-    store_early = pltpu.make_async_copy(
-        o_buf.at[pl.ds(0, block)], att_hbm.at[pl.ds(0, block)], out_sem.at[1]
-    )
-    store_early.start()
     for j in range(steps):
         stage4(j)
     for copy in sent:
         copy.wait_send()
-    store_late.wait()
-    store_early.wait()
 
 
 def on_device(
@@ -412,7 +411,7 @@
     rows = n * count
     zs = n // 4
     wide = (fe // LANES) * LANES + up_to(fe, TILE) + LANES
-    pieces = len(cuts(d, 6 * LANES))
+    pieces = len(cuts(d, 12 * LANES))
     vmem = pl.BlockSpec(memory_space=pltpu.VMEM)
     smem = pl.BlockSpec(memory_space=pltpu.SMEM)
     hbm = pl.BlockSpec(memory_space=pl.ANY)
@@ -420,13 +419,12 @@
     return pl.pallas_call(
         functools.partial(kernel, n),
         out_shape=(
-            jax.ShapeDtypeStruct(query_proj.shape, BF16),
-            jax.ShapeDtypeStruct(routed_stream.shape, BF16),
+            pltpu.VMEM(query_proj.shape, BF16),
+            pltpu.VMEM(routed_stream.shape, BF16),
         ),
         in_specs=[hbm, hbm, hbm, vmem, smem, vmem, vmem, vmem, hbm, hbm],
-        out_specs=(hbm, vmem),
+        out_specs=(vmem, vmem),
         scratch_shapes=[
-            pltpu.VMEM(query_proj.shape, BF16),
             pltpu.VMEM(query_proj.shape, BF16),
             pltpu.VMEM((WINDOW + length, kv), BF16),
             pltpu.VMEM((WINDOW + length, kv), BF16),
@@ -462,7 +460,6 @@
             dma((pieces,)),
             dma((pieces * (zs - 1),)),
             dma((pieces * (zs - 1),)),
-            dma((2,)),
         ],
         compiler_params=pltpu.CompilerParams(
             collective_id=0, has_side_effects=True, vmem_limit_bytes=58 * 2**20
@@ -474,8 +471,8 @@
         call_ids.reshape(1, length),
         sink_logits,
         routed_stream,
-        expert_ids,
-        route_weights,
+        expert_ids.T,
+        route_weights.T,
         gate_up[0],
         down_proj[0],
     )

time: 57 us -> 49.9 us (0.88)
  local copies, waits for them, and re-layouts: 6.52 us -> 1.96 us
  Pallas kernels: 49.6 us -> 47.1 us
    unnamed x6 -> x2, local copies, waits for them, and re-layouts: 6.52 us -> 1.96 us
    pallas_call x1, Pallas kernels: 49.6 us -> 47.1 us  [on_device(): pl.pallas_call(functools.partial(kernel, n), out_shape=(pltpu.VMEM(query_...]
where the time goes in v2:
time: 49.9 us; the launch traced here: 49.7 us
  Pallas kernels  47.1 us (94%)
  local copies, waits for them, and re-layouts  1.96 us (4%)
  between operations  0.64 us (1%)
    pallas_call x1, Pallas kernels, on_device(): pl.pallas_call(functools.partial(kernel, n), out_shape=(pltpu.VMEM(query_...  47.1 us
    unnamed x2, local copies, waits for them, and re-layouts  1.96 us

profile of v2, /device:TPU:0, one launch (start us, length us, event | category | flops | bytes accessed | tf_op | source)
XLA Modules:
  0.0 49.7 jit_solution(8248506409745533672)
XLA Ops:
  0.6 47.1 %shard_map.113 = (bf16[256,4096]{1,0:T(8,128)(2,1)S(1)}, bf16[16,2880]{1,0:T(8,128)(2,1)S(1)}) custom-call(bf16[256,4096]{1,0:T(8,128)(2,1)} %q_hbm.1, bf16[256,512]{1,0:T(8,128)(2,1)} %k_hbm.1, bf16[256,512]{1,0:T(8,128)(2,1)} %v_hbm.1, s32[1,256]{1,0:T(1,128)} %bitcast.9, f32[64]{0:T(128)} %sink_ref.1, bf16[16,2880]{1,0:T(8,128)(2,1)} %routed_ref.1, ...), custom_call_target="tpu_custom_call" | custom-call | tf_op jit(solution)/shard_map/pallas_call | solution.py:419
  47.8 1.3 %copy.14 = bf16[256,4096]{1,0:T(8,128)(2,1)} copy(bf16[256,4096]{1,0:T(8,128)(2,1)S(1)} %get-tuple-element.2) | data formatting | bytes 4194304
  49.1 0.6 %copy.15 = bf16[16,2880]{1,0:T(8,128)(2,1)} copy(bf16[16,2880]{1,0:T(8,128)(2,1)S(1)} %get-tuple-element.3) | data formatting | bytes 184320

commit v3 on v2

--- a/solution.py
+++ b/solution.py
@@ -279,16 +279,6 @@
         send(slot(0, 1, zr), slot(1, 1, zr), c_send.at[zs + k], arrival(1, 1, zr), sibling)
     for copy in gate_loads + down_loads:
         copy.wait()
-    loads[3].wait()
-    arrived(k_cat.at[head], halo_recv.at[0])
-    arrived(v_cat.at[head], halo_recv.at[1])
-    arrived(calls_in, halo_recv.at[2])
-    make_bias(
-        0,
-        jnp.concatenate([calls_in[0:1, :], own_calls[:, :block]], axis=1),
-        own_calls[:, :block],
-        me > 0,
-    )
     for yr in range(2):
         for zr in range(zs):
             arrived(slot(1, yr, zr), arrival(1, yr, zr))
@@ -375,6 +365,16 @@
         if j:
             stage2(j - 1)
     stage2(len(pieces) - 1)
+    loads[3].wait()
+    arrived(k_cat.at[head], halo_recv.at[0])
+    arrived(v_cat.at[head], halo_recv.at[1])
+    arrived(calls_in, halo_recv.at[2])
+    make_bias(
+        0,
+        jnp.concatenate([calls_in[0:1, :], own_calls[:, :block]], axis=1),
+        own_calls[:, :block],
+        me > 0,
+    )
     steps = len(pieces)
     done = 0
     for g in range(groups // 2):

time: 49.9 us -> 49.9 us (level)
  no operation moved by 1% of the time
where the time goes in v3:
time: 49.9 us; the launch traced here: 49.7 us
  Pallas kernels  47.1 us (94%)
  local copies, waits for them, and re-layouts  1.96 us (4%)
  between operations  0.64 us (1%)
    pallas_call x1, Pallas kernels, on_device(): pl.pallas_call(functools.partial(kernel, n), out_shape=(pltpu.VMEM(query_...  47.1 us
    unnamed x2, local copies, waits for them, and re-layouts  1.96 us

profile of v3, /device:TPU:0, one launch (start us, length us, event | category | flops | bytes accessed | tf_op | source)
XLA Modules:
  0.0 49.7 jit_solution(3753113240004732383)
XLA Ops:
  0.6 47.1 %shard_map.113 = (bf16[256,4096]{1,0:T(8,128)(2,1)S(1)}, bf16[16,2880]{1,0:T(8,128)(2,1)S(1)}) custom-call(bf16[256,4096]{1,0:T(8,128)(2,1)} %q_hbm.1, bf16[256,512]{1,0:T(8,128)(2,1)} %k_hbm.1, bf16[256,512]{1,0:T(8,128)(2,1)} %v_hbm.1, s32[1,256]{1,0:T(1,128)} %bitcast.9, f32[64]{0:T(128)} %sink_ref.1, bf16[16,2880]{1,0:T(8,128)(2,1)} %routed_ref.1, ...), custom_call_target="tpu_custom_call" | custom-call | tf_op jit(solution)/shard_map/pallas_call | solution.py:419
  47.8 1.3 %copy.14 = bf16[256,4096]{1,0:T(8,128)(2,1)} copy(bf16[256,4096]{1,0:T(8,128)(2,1)S(1)} %get-tuple-element.2) | data formatting | bytes 4194304
  49.1 0.6 %copy.15 = bf16[16,2880]{1,0:T(8,128)(2,1)} copy(bf16[16,2880]{1,0:T(8,128)(2,1)S(1)} %get-tuple-element.3) | data formatting | bytes 184320
